TPU v7x, 32 devices: a whole 2x2x4 slice. The times are simulated.
32 devices in a mesh: dom: 8 (over y, x, core), shard: 4 (over z).
Axes of the slice: x: 2, y: 2, z: 4, core: 2. Of those that a mesh axis runs over, the one named last changes fastest.
Arguments:
- lhs_emb: bfloat16 [8192, 400], P(('dom', 'shard')), may hold values from -4 to 4
- lhs_acc: float32 [8192], P(('dom', 'shard')), may hold values from 0.05 to 1
- rhs_emb: bfloat16 [8192, 400], P(('dom', 'shard')), may hold values from -4 to 4
- rhs_acc: float32 [8192], P(('dom', 'shard')), may hold values from 0.05 to 1
- operators: float32 [2, 400, 400], replicated, may hold values from -2 to 2
- operator_acc: float32 [2, 400], replicated, may hold values from 65.536 to 1966.08
- partner_mask: int32 [1], replicated, may hold values from 1 to 7
- edge_lhs: int32 [512, 128], P(('dom', 'shard')), may hold values from 0 to 1023
- edge_rhs: int32 [512, 128], P(('dom', 'shard')), may hold values from 0 to 1023
- negatives: int32 [512, 128], P(('dom', 'shard')), may hold values from 0 to 1023
- block_relation: int32 [512], P(('dom', 'shard')), may hold values from 0 to 1
- edge_count: int32 [32], P(('dom', 'shard')), may hold values from 1 to 2048, as said below
Outputs:
- new_lhs: bfloat16 [8192, 400], P(('dom', 'shard'))
- new_lhs_acc: float32 [8192], P(('dom', 'shard'))
- new_rhs: bfloat16 [8192, 400], P(('dom', 'shard'))
- new_rhs_acc: float32 [8192], P(('dom', 'shard'))
- new_operators: float32 [2, 400, 400], replicated
- new_operator_acc: float32 [2, 400], replicated
Inputs may be any that keep to these rules, and one draw needn't show every extreme that they name: `edge_count`: the live edges of a device fill the first slots of its blocks, block after block; in every draw some device is full with 2048 live edges.
All inputs are finite; a program needn't handle non-finite values.
Results may differ from a plain program's by a relative error of at most 0.0058.
Values may be sent and summed in bfloat16 or wider, within the bound.
A program may use at most 64 MiB of HBM per device.

v0:
```python
import jax
import jax.numpy as jnp
from jax import lax
from jax.sharding import PartitionSpec as P

D = 400
SPAN = 128


LEARN_RATE = 0.1


def from_partner(array, axis, distance):
    return lax.ppermute(array, axis, [(i, i ^ 1 << distance) for i in range(lax.axis_size(axis))])


def block_terms(left_rows, candidates, operator_low, live_count):
    projected = jnp.dot(left_rows, operator_low, preferred_element_type=jnp.float32).astype(
        jnp.bfloat16
    )
    scores = lax.dot_general(
        projected, candidates, (((1,), (1,)), ((), ())), preferred_element_type=jnp.float32
    )
    positions = jnp.arange(left_rows.shape[0], dtype=jnp.int32)
    columns = jnp.arange(candidates.shape[0], dtype=jnp.int32)
    column_live = (columns < live_count) | (columns >= left_rows.shape[0])
    row_live = positions < live_count
    masked = jnp.where(column_live[None, :], scores, -jnp.inf)
    row_top = jnp.max(masked, axis=1, keepdims=True)
    exp_scores = jnp.exp(masked - row_top)
    soft_weights = exp_scores / jnp.sum(exp_scores, axis=1, keepdims=True)
    target = (positions[:, None] == columns[None, :]).astype(jnp.float32)
    score_grad = ((soft_weights - target) * row_live[:, None].astype(jnp.float32)).astype(
        jnp.bfloat16
    )
    proj_grad = jnp.dot(score_grad, candidates, preferred_element_type=jnp.float32).astype(
        jnp.bfloat16
    )
    cand_grad = lax.dot_general(
        score_grad, projected, (((0,), (0,)), ((), ())), preferred_element_type=jnp.float32
    )
    left_grad = lax.dot_general(
        proj_grad, operator_low, (((1,), (1,)), ((), ())), preferred_element_type=jnp.float32
    )
    oper_grad = lax.dot_general(
        left_rows, proj_grad, (((0,), (0,)), ((), ())), preferred_element_type=jnp.float32
    )
    return (left_grad, cand_grad, oper_grad)


def row_adagrad(weights_in, state_in, grad_in):
    new_state = state_in + jnp.mean(grad_in * grad_in, axis=-1)
    updated = weights_in.astype(jnp.float32) - LEARN_RATE * grad_in / jnp.sqrt(new_state)[..., None]
    return (updated, new_state)


def level_flag(partner_bits, level_bit):
    return jnp.bitwise_and(jnp.right_shift(partner_bits, level_bit), 1) == 1


def fetch_rows(block_rows, partner_bits):
    groups = lax.axis_size("dom")
    for level_bit in range(groups.bit_length() - 1):
        swapped = from_partner(block_rows, "dom", level_bit)
        block_rows = jnp.where(level_flag(partner_bits, level_bit), swapped, block_rows)
    return block_rows


def return_rows(block_rows, partner_bits):
    groups = lax.axis_size("dom")
    for level_bit in range(groups.bit_length() - 1):
        swapped = from_partner(block_rows.astype(jnp.bfloat16), "dom", level_bit).astype(
            block_rows.dtype
        )
        block_rows = jnp.where(level_flag(partner_bits, level_bit), swapped, block_rows)
    return block_rows


def per_device(
    lhs_emb,
    lhs_acc,
    rhs_emb,
    rhs_acc,
    operators,
    operator_acc,
    partner_mask,
    edge_lhs,
    edge_rhs,
    negatives,
    block_relation,
    edge_count,
):
    partner_bits = partner_mask[0]
    fetched = fetch_rows(rhs_emb, partner_bits)
    left_part, right_part = (
        lax.all_gather(lhs_emb, "shard", axis=0, tiled=True),
        lax.all_gather(fetched, "shard", axis=0, tiled=True),
    )
    operator_low = operators.astype(jnp.bfloat16)

    def add_block(running, left_index, right_index, neg_index, relation, live_count):
        grad_left, grad_right, grad_oper = running
        cand_index = jnp.concatenate([right_index, neg_index])
        left_rows = jnp.take(left_part, left_index, axis=0)
        candidates = jnp.take(right_part, cand_index, axis=0)
        left_grad, cand_grad, oper_grad = block_terms(
            left_rows, candidates, operator_low[relation], live_count
        )
        return (
            grad_left.at[left_index].add(left_grad),
            grad_right.at[cand_index].add(cand_grad),
            grad_oper.at[relation].add(oper_grad),
        )

    zeros_rows = jnp.zeros((left_part.shape[0], D), jnp.float32)
    initial = (zeros_rows, zeros_rows, jnp.zeros(operators.shape, jnp.float32))
    live_edges = edge_count[0]

    def visit_own(block_index, running):
        return add_block(
            running,
            edge_lhs[block_index],
            edge_rhs[block_index],
            negatives[block_index],
            block_relation[block_index],
            live_edges - block_index * SPAN,
        )

    gradients = lax.fori_loop(jnp.int32(0), (live_edges + SPAN - 1) // SPAN, visit_own, initial)
    grad_left, grad_right, grad_oper = gradients
    own_left, own_right = (
        lax.psum_scatter(
            grad_left.astype(jnp.bfloat16), "shard", scatter_dimension=0, tiled=True
        ).astype(jnp.float32),
        lax.psum_scatter(
            grad_right.astype(jnp.bfloat16), "shard", scatter_dimension=0, tiled=True
        ).astype(jnp.float32),
    )
    owner_right = return_rows(own_right, partner_bits)
    new_lhs, new_lhs_acc = row_adagrad(lhs_emb, lhs_acc, own_left)
    new_rhs, new_rhs_acc = row_adagrad(rhs_emb, rhs_acc, owner_right)
    total_oper = lax.psum(grad_oper, ("dom", "shard"))
    new_operators, new_operator_acc = row_adagrad(operators, operator_acc, total_oper)
    return (
        new_lhs.astype(jnp.bfloat16),
        new_lhs_acc,
        new_rhs.astype(jnp.bfloat16),
        new_rhs_acc,
        new_operators,
        new_operator_acc,
    )


def solution(mesh):
    in_specs = (
        P(("dom", "shard"), None),
        P(("dom", "shard")),
        P(("dom", "shard"), None),
        P(("dom", "shard")),
        P(),
        P(),
        P(),
        P(("dom", "shard"), None),
        P(("dom", "shard"), None),
        P(("dom", "shard"), None),
        P(("dom", "shard")),
        P(("dom", "shard")),
    )
    out_specs = (
        P(("dom", "shard"), None),
        P(("dom", "shard")),
        P(("dom", "shard"), None),
        P(("dom", "shard")),
        P(),
        P(),
    )
    return jax.shard_map(
        per_device, mesh=mesh, in_specs=in_specs, out_specs=out_specs, check_vma=False
    )
```

profile of v0, /device:TPU:0, one launch (start us, length us, event | category | flops | bytes accessed | tf_op | source)
XLA Modules:
  0.0 678.3 jit_solution(9589542146367575995)
XLA Ops:
  9.9 1.0 broadcast_select_fusion.6
  10.8 2.9 collective-permute-start.1
  14.4 1.1 copy.24
  15.5 2.4 convert_element_type.64
  17.9 1.2 collective-permute-done.1
  19.1 1.8 collective-permute-start.2
  21.0 23.3 %all_gather.6 = bf16[1024,400]{1,0:T(8,128)(2,1)} all-gather(bf16[256,400]{1,0:T(8,128)(2,1)S(1)} %copy.24), channel_id=1, replica_groups=mesh['dom'=8,'shard'=4] {'shard'}, dimensions={0}, use_global_device_ids=true | all-gather | bytes 1024000 | tf_op jit(solution)/shard_map/all_gather | solution.py:96
  44.4 17.7 %all_gather.7 = bf16[1024,400]{0,1:T(8,128)(2,1)S(1)} all-gather(bf16[256,400]{0,1:T(8,128)(2,1)S(1)} %broadcast_select_fusion.8), channel_id=1, replica_groups=mesh['dom'=8,'shard'=4] {'shard'}, dimensions={0}, use_global_device_ids=true | all-gather | bytes 1024000 | tf_op jit(solution)/shard_map/all_gather | solution.py:97
  62.5 1.4 broadcast_in_dim.51
  64.2 1.6 broadcast_in_dim.50
  65.8 27.6 %while.15 = (s32[]{:T(128)}, f32[1024,400]{1,0:T(8,128)}, f32[1024,400]{1,0:T(8,128)S(1)}, f32[2,400,400]{2,1,0:T(8,128)}, s32[]{:T(128)}, /*index=5*/s32[16,128...) while((s32[]{:T(128)}, f32[1024,400]{1,0:T(8,128)}, ...), condition=%wide.region_6.7_spmd, body=%wide.region_0.6_spmd.sunk | while | flops 203003024 | bytes 10283850 | solution.py:129
  69.0 0.8 and_reduce_fusion.2
  71.9 2.2 gather_fusion.1
  74.2 1.4 convolution_convert_fusion.4
  75.6 1.9 gather_fusion
  77.4 1.4 fusion.56
  79.0 1.3 convolution_convert_fusion.5
  80.7 2.1 fusion.59
  82.7 3.0 fusion.60
  85.8 3.4 scatter_fusion.1
  89.2 4.2 scatter_fusion
  93.4 1.3 copy.27
  94.9 2.5 copy.26
  97.4 551.1 %all-reduce.2.cloned.1.call-done = f32[2,400,400]{2,1,0:T(8,128)} async-done(((f32[2,400,400]{2,1,0:T(8,128)}), f32[2,400,400]{2,1,0:T(8,128)}) %all-reduce.2.cloned.1.call-update) | async-done | bytes 1280016 | tf_op jit(solution)/shard_map/psum | solution.py:142
  648.5 1.7 multiply_reduce_fusion
  650.8 2.9 divide_subtract_fusion
  653.7 1.1 fusion.24
  654.9 1.4 collective-permute-start.4
  656.9 5.5 collective-permute-done.4
  662.5 1.4 collective-permute-start.5
  664.7 4.6 collective-permute-done.5
  670.0 0.9 subtract_convert_fusion
  (64 shorter events, 8.2 us)
Async XLA Ops:
  8.0 640.5 %all-reduce.2.cloned.1.call-start = ((), (), s32[]{:S(2)}) async-start(), calls=%async_computation.4 | async-start | bytes 3276800 | tf_op jit(solution)/shard_map/psum | solution.py:142
  8.0 1.8 collective-permute-start
  10.8 8.3 %collective-permute-start.1 = (bf16[256,400]{0,1:T(8,128)(2,1)S(1)}, bf16[256,400]{0,1:T(8,128)(2,1)S(1)}, u32[]{:S(2)}, u32[]{:S(2)}) collective-permute-start(bf16[256,400]{0,1:T(8,128)(2,1)S(1)} %broadcast_select_fusion.6), channel_id=1, source_target_pairs={{0,8},{4,12},{8,0},{12,4},{16,24},{20,28},{24,16},{28,20},{1,9},{5... | collective-permute-start | bytes 614408 | tf_op jit(solution)/shard_map/ppermute | solution.py:14
  19.1 25.2 %collective-permute-start.2 = (bf16[256,400]{0,1:T(8,128)(2,1)S(1)}, bf16[256,400]{0,1:T(8,128)(2,1)S(1)}, u32[]{:S(2)}, u32[]{:S(2)}) collective-permute-start(bf16[256,400]{0,1:T(8,128)(2,1)S(1)} %broadcast_select_fusion.7), channel_id=1, source_target_pairs={{0,16},{4,20},{8,24},{12,28},{16,0},{20,4},{24,8},{28,12},{1,17},{... | collective-permute-start | bytes 614408 | tf_op jit(solution)/shard_map/ppermute | solution.py:14
  63.9 1.9 copy-start.7
  63.9 1.9 copy-start.12
  71.1 7.9 %copy-start.8 = (f32[128]{0:T(128)}, f32[128]{0:T(128)S(1)}, u32[]{:S(2)}) copy-start(f32[128]{0:T(128)S(1)} %compare_convert_fusion.2) | copy-start | bytes 1540 | tf_op jit(solution)/shard_map/while
  75.6 3.5 copy-start.1
  77.4 2.9 copy-start
  89.1 4.2 copy-start.13
  93.4 557.3 %reduce-scatter.5.cloned.1.call-start = ((), (), s32[]{:S(2)}) async-start(), calls=%async_computation.3 | async-start | bytes 1024000 | tf_op jit(solution)/shard_map/reduce_scatter | solution.py:135
  94.8 558.9 %reduce-scatter.3.cloned.1.call-start = ((), (), s32[]{:S(2)}) async-start(), calls=%async_computation.2 | async-start | bytes 1024000 | tf_op jit(solution)/shard_map/reduce_scatter | solution.py:132
  97.3 552.8 %copy-start.9 = (f32[2,400]{1,0:T(2,128)S(1)}, f32[2,400]{1,0:T(2,128)}, u32[]{:S(2)}) copy-start(f32[2,400]{1,0:T(2,128)} %param.21) | copy-start | bytes 9604
  97.3 553.4 %copy-start.2 = (f32[2,400,400]{2,1,0:T(8,128)S(1)}, f32[2,400,400]{2,1,0:T(8,128)}, u32[]{:S(2)}) copy-start(f32[2,400,400]{2,1,0:T(8,128)} %param.20) | copy-start | bytes 3840004
  650.7 4.1 collective-permute-start.3
  650.7 4.1 copy-start.3
  650.7 5.6 copy-start.10
  653.7 10.3 %copy-start.4 = (bf16[256,400]{0,1:T(8,128)(2,1)S(1)}, bf16[256,400]{0,1:T(8,128)(2,1)}, u32[]{:S(2)}) copy-start(bf16[256,400]{0,1:T(8,128)(2,1)} %param.16) | copy-start | bytes 614404
  653.7 15.7 %copy-start.11 = (f32[256]{0:T(256)S(1)}, f32[256]{0:T(256)}, u32[]{:S(2)}) copy-start(f32[256]{0:T(256)} %param.19) | copy-start | bytes 3076
  653.7 16.3 %copy-start.6 = (bf16[256,400]{0,1:T(8,128)(2,1)S(1)}, bf16[256,400]{0,1:T(8,128)(2,1)}, u32[]{:S(2)}) copy-start(bf16[256,400]{0,1:T(8,128)(2,1)} %param.18) | copy-start | bytes 614404
  653.7 10.2 %copy-start.5 = (bf16[256,400]{0,1:T(8,128)(2,1)S(1)}, bf16[256,400]{0,1:T(8,128)(2,1)}, u32[]{:S(2)}) copy-start(bf16[256,400]{0,1:T(8,128)(2,1)} %reduce-scatter.3.cloned.1.call-done) | copy-start | bytes 614404
  654.9 7.5 %collective-permute-start.4 = (bf16[256,400]{0,1:T(8,128)(2,1)S(1)}, bf16[256,400]{0,1:T(8,128)(2,1)S(1)}, u32[]{:S(2)}, u32[]{:S(2)}) collective-permute-start(bf16[256,400]{0,1:T(8,128)(2,1)S(1)} %fusion.25), channel_id=1, source_target_pairs={{0,8},{4,12},{8,0},{12,4},{16,24},{20,28},{24,16},{28,20},{1,9},{5... | collective-permute-start | bytes 614408 | tf_op jit(solution)/shard_map/ppermute | solution.py:14
  662.5 6.8 collective-permute-start.5
Sparse Core Ops, SparseCore 0:
  93.5 554.9 all-reduce.1
Sparse Core Ops, SparseCore 1:
  96.2 438.5 reduce-scatter.4
  536.9 23.4 reduce-scatter.2
where the time goes:
time: 685 us; the launch traced here: 678 us
  waiting for transfers between devices  563 us (82%)
  blocking collectives  41 us (6%)
  other arithmetic  22.7 us (3%)
  between operations  16.9 us (2%)
  local copies, waits for them, and re-layouts  14.1 us (2%)
  matrix products  9.5 us (1%)
  starting transfers between devices  8.28 us (1%)
    psum x1, waiting for transfers between devices, per_device(): total_oper = lax.psum(grad_oper, ('dom', 'shard'))  551 us
    all_gather x1, blocking collectives, per_device(): lax.all_gather(lhs_emb, 'shard', axis=0, tiled=True)  23.3 us
    all_gather x1, blocking collectives, per_device(): lax.all_gather(fetched, 'shard', axis=0, tiled=True)  17.7 us
  transfers between devices with their start and end apart: 9, of which 5 were waited for; matrix products, arithmetic and copies ran while one was open for 2% of the time, Pallas kernels for 0%

commit v1 on v0

v1 whole, which is shorter than its diff:
```python
import functools

import jax
import jax.numpy as jnp
from jax import lax
from jax.experimental import pallas as pl
from jax.experimental.pallas import tpu as pltpu
from jax.sharding import PartitionSpec as P

D = 400
WIDE = 512
SPAN = 128
LEARN_RATE = 0.1
BF = jnp.bfloat16
F32 = jnp.float32


def from_partner(array, axis, distance):
    return lax.ppermute(array, axis, [(i, i ^ 1 << distance) for i in range(lax.axis_size(axis))])


def row_adagrad(weights_in, state_in, grad_in):
    new_state = state_in + jnp.mean(grad_in * grad_in, axis=-1)
    updated = weights_in.astype(F32) - LEARN_RATE * grad_in / jnp.sqrt(new_state)[..., None]
    return (updated, new_state)


def level_flag(partner_bits, level_bit):
    return jnp.bitwise_and(jnp.right_shift(partner_bits, level_bit), 1) == 1


def move_rows(block_rows, partner_bits):
    groups = lax.axis_size("dom")
    for level_bit in range(groups.bit_length() - 1):
        swapped = from_partner(block_rows, "dom", level_bit)
        block_rows = jnp.where(level_flag(partner_bits, level_bit), swapped, block_rows)
    return block_rows


def dot(a, b, dims):
    return lax.dot_general(a, b, (dims, ((), ())), preferred_element_type=F32)


def as_column(index_row):
    return jnp.transpose(jnp.broadcast_to(index_row, (128, index_row.shape[1])))


def gather_rows(index_row, table):
    part = table.shape[0]
    column = as_column(index_row)
    lanes = lax.broadcasted_iota(jnp.int32, column.shape, 1)
    shifted = column - lanes
    hot = jnp.concatenate(
        [jnp.where(shifted == c * 128, 1.0, 0.0).astype(BF) for c in range(part // 128)], axis=1
    )
    return dot(hot, table[...], ((1,), (0,))).astype(BF)


def scatter_rows(index_row, grads, total):
    part = total.shape[0]
    step = 256
    rows = lax.broadcasted_iota(jnp.int32, (step, index_row.shape[1]), 0)
    shifted = jnp.broadcast_to(index_row, rows.shape) - rows
    for c in range(part // step):
        hot = jnp.where(shifted == c * step, 1.0, 0.0).astype(BF)
        total[pl.ds(c * step, step), :] += dot(hot, grads, ((1,), (0,)))


def bucket_kernel(
    groups,
    blocks,
    info,
    index,
    left_in,
    right_in,
    oper_in,
    left_out,
    right_out,
    oper_out,
    left,
    right,
    oper,
    left_sum,
    right_sum,
    oper_sum,
):
    me = lax.axis_index("shard")
    for wide, narrow in ((left, left_in), (right, right_in)):
        wide[:, 384:] = jnp.zeros((wide.shape[0], WIDE - 384), BF)
        wide[:, :D] = narrow[...]
    oper[...] = jnp.zeros_like(oper)
    oper[:, :D, :D] = oper_in[...].astype(BF)
    left_sum[...] = jnp.zeros_like(left_sum)
    right_sum[...] = jnp.zeros_like(right_sum)
    oper_sum[...] = jnp.zeros_like(oper_sum)

    counts = [info[g * blocks, 1] for g in range(groups)]
    starts = [jnp.int32(0)]
    for g in range(groups):
        starts.append(starts[-1] + (counts[g] + SPAN - 1) // SPAN)
    in_all = starts[-1]
    mine = (in_all - me + groups - 1) // groups

    def locate(step):
        slot = step * groups + me
        exists = slot < in_all
        slot = jnp.minimum(slot, in_all - 1)
        owner = jnp.int32(0)
        start = jnp.int32(0)
        count = counts[0]
        for g in range(1, groups):
            later = slot >= starts[g]
            owner = jnp.where(later, g, owner)
            start = jnp.where(later, starts[g], start)
            count = jnp.where(later, counts[g], count)
        within = slot - start
        flat = owner * blocks + within
        live = jnp.where(exists, count - within * SPAN, 0)
        return flat, info[flat, 0], live

    def visit(pair, carry):
        left_ids, right_ids, left_grads, right_grads = [], [], [], []
        for half in range(2):
            flat, relation, live = locate(pair * 2 + half)
            row = index[pl.ds(flat, 1), :]
            left_id = row[:, :SPAN]
            right_id = row[:, SPAN : 3 * SPAN]
            low = oper[relation]
            left_rows = gather_rows(left_id, left)
            candidates = gather_rows(right_id, right)
            projected = dot(left_rows, low, ((1,), (0,))).astype(BF)
            scores = dot(projected, candidates, ((1,), (1,)))
            rows = lax.broadcasted_iota(jnp.int32, scores.shape, 0)
            columns = lax.broadcasted_iota(jnp.int32, scores.shape, 1)
            column_live = (columns < live) | (columns >= SPAN)
            masked = jnp.where(column_live, scores, -jnp.inf)
            row_top = jnp.max(masked, axis=1, keepdims=True)
            exp_scores = jnp.exp(masked - row_top)
            soft = exp_scores / jnp.sum(exp_scores, axis=1, keepdims=True)
            grad = soft - jnp.where(rows == columns, 1.0, 0.0)
            score_grad = jnp.where(rows < live, grad, 0.0).astype(BF)
            proj_grad = dot(score_grad, candidates, ((1,), (0,))).astype(BF)
            cand_grad = dot(score_grad, projected, ((0,), (0,)))
            left_grad = dot(proj_grad, low, ((1,), (1,)))
            oper_sum[relation] += dot(left_rows, proj_grad, ((0,), (0,)))
            left_ids.append(left_id)
            right_ids.append(right_id)
            left_grads.append(left_grad.astype(BF))
            right_grads.append(cand_grad.astype(BF))
        join = lambda parts, axis: jnp.concatenate(parts, axis=axis)
        scatter_rows(join(left_ids, 1), join(left_grads, 0), left_sum)
        scatter_rows(join(right_ids, 1), join(right_grads, 0), right_sum)
        return carry

    lax.fori_loop(0, (mine + 1) // 2, visit, 0)
    left_out[...] = left_sum[:, :D].astype(BF)
    right_out[...] = right_sum[:, :D].astype(BF)
    oper_out[...] = oper_sum[:, :D, :D]


def bucket(packed, left_part, right_part, operators):
    groups = lax.axis_size("shard")
    total, _ = packed.shape
    part = left_part.shape[0]
    whole = lambda shape: pl.BlockSpec(shape, lambda i: (0,) * len(shape))
    nrel = operators.shape[0]
    return pl.pallas_call(
        functools.partial(bucket_kernel, groups, total // groups),
        grid=(1,),
        in_specs=[
            pl.BlockSpec((total, 128), lambda i: (0, 3), memory_space=pltpu.SMEM),
            whole(packed.shape),
            whole(left_part.shape),
            whole(right_part.shape),
            whole(operators.shape),
        ],
        out_specs=[whole((part, D)), whole((part, D)), whole(operators.shape)],
        out_shape=[
            jax.ShapeDtypeStruct((part, D), BF),
            jax.ShapeDtypeStruct((part, D), BF),
            jax.ShapeDtypeStruct(operators.shape, F32),
        ],
        scratch_shapes=[
            pltpu.VMEM((part, WIDE), BF),
            pltpu.VMEM((part, WIDE), BF),
            pltpu.VMEM((nrel, WIDE, WIDE), BF),
            pltpu.VMEM((part, WIDE), F32),
            pltpu.VMEM((part, WIDE), F32),
            pltpu.VMEM((nrel, WIDE, WIDE), F32),
        ],
        compiler_params=pltpu.CompilerParams(vmem_limit_bytes=48 * 1024 * 1024),
        name="bucket",
    )(packed, packed, left_part, right_part, operators)


def per_device(
    lhs_emb,
    lhs_acc,
    rhs_emb,
    rhs_acc,
    operators,
    operator_acc,
    partner_mask,
    edge_lhs,
    edge_rhs,
    negatives,
    block_relation,
    edge_count,
):
    partner_bits = partner_mask[0]
    blocks = block_relation.shape[0]
    lane = lax.broadcasted_iota(jnp.int32, (blocks, 128), 1)
    info = jnp.where(lane == 0, block_relation[:, None], edge_count[0])
    packed = jnp.concatenate([edge_lhs, edge_rhs, negatives, info], axis=1)
    packed = lax.all_gather(packed, "shard", axis=0, tiled=True)
    left_part = lax.all_gather(lhs_emb, "shard", axis=0, tiled=True)
    fetched = move_rows(rhs_emb, partner_bits)
    right_part = lax.all_gather(fetched, "shard", axis=0, tiled=True)
    grad_left, grad_right, grad_oper = bucket(packed, left_part, right_part, operators)
    own_left, own_right = (
        lax.psum_scatter(g, "shard", scatter_dimension=0, tiled=True)
        for g in (grad_left, grad_right)
    )
    owner_right = move_rows(own_right, partner_bits)
    new_lhs, new_lhs_acc = row_adagrad(lhs_emb, lhs_acc, own_left.astype(F32))
    new_rhs, new_rhs_acc = row_adagrad(rhs_emb, rhs_acc, owner_right.astype(F32))
    total_oper = lax.psum(grad_oper, ("dom", "shard"))
    new_operators, new_operator_acc = row_adagrad(operators, operator_acc, total_oper)
    return (
        new_lhs.astype(BF),
        new_lhs_acc,
        new_rhs.astype(BF),
        new_rhs_acc,
        new_operators,
        new_operator_acc,
    )


def solution(mesh):
    rows = P(("dom", "shard"), None)
    flat = P(("dom", "shard"))
    in_specs = (rows, flat, rows, flat, P(), P(), P(), rows, rows, rows, flat, flat)
    out_specs = (rows, flat, rows, flat, P(), P())
    return jax.shard_map(
        per_device, mesh=mesh, in_specs=in_specs, out_specs=out_specs, check_vma=False
    )
```

time: 685 us -> 280 us (0.41); the launches traced: 678 us -> 281 us
  waiting for transfers between devices: 563 us -> 159 us
  Pallas kernels: 0 us -> 30 us
  other arithmetic: 22.7 us -> 8.49 us
  blocking collectives: 41 us -> 54.5 us
  local copies, waits for them, and re-layouts: 14.1 us -> 3.82 us
  matrix products: 9.5 us -> 0 us
    psum x1, waiting for transfers between devices: 551 us -> 146 us  [per_device(): total_oper = lax.psum(grad_oper, ('dom', 'shard'))]
    pallas_call x0 -> x1, Pallas kernels: none -> 30 us  [bucket(): pl.pallas_call(functools.partial(bucket_kernel, groups, total // groups),...]
    all_gather x2 -> x3, blocking collectives: 41 us -> 54.5 us  [the longest x1 22.2 us: per_device(): left_part = lax.all_gather(lhs_emb, 'shard', axis=0, tiled=True)]
    dot_general x6 -> x0, matrix products: 9.5 us -> none  [the longest x1 3.04 us: block_terms(): lax.dot_general(left_rows, proj_grad, (((0,), (0,)), ((), ())), preferred...]
    scatter-add x2 -> x0, other arithmetic: 7.57 us -> none  [the longest x1 4.21 us: add_block(): grad_left.at[left_index].add(left_grad)]
  transfers between devices with their start and end apart: 9 -> 9, of which waited for: 5 -> 3; matrix products, arithmetic and copies ran while one was open for 2% -> 3% of each run, Pallas kernels for 0% -> 0%
where the time goes in v1:
time: 280 us; the launch traced here: 281 us
  waiting for transfers between devices  159 us (57%)
  blocking collectives  54.5 us (19%)
  Pallas kernels  30 us (11%)
  between operations  17 us (6%)
  other arithmetic  8.49 us (3%)
  starting transfers between devices  7.86 us (3%)
  local copies, waits for them, and re-layouts  3.82 us (1%)
    psum x1, waiting for transfers between devices, per_device(): total_oper = lax.psum(grad_oper, ('dom', 'shard'))  146 us
    pallas_call x1, Pallas kernels, bucket(): pl.pallas_call(functools.partial(bucket_kernel, groups, total // groups),...  30 us
    all_gather x1, blocking collectives, per_device(): left_part = lax.all_gather(lhs_emb, 'shard', axis=0, tiled=True)  22.2 us
    all_gather x1, blocking collectives, per_device(): right_part = lax.all_gather(fetched, 'shard', axis=0, tiled=True)  18.6 us
    all_gather x1, blocking collectives, per_device(): packed = lax.all_gather(packed, 'shard', axis=0, tiled=True)  13.6 us
    ppermute x6, waiting for transfers between devices, from_partner(): lax.ppermute(array, axis, [(i, i ^ 1 << distance) for i in range(lax.axis...  12.3 us
    ppermute x6, starting transfers between devices, from_partner(): lax.ppermute(array, axis, [(i, i ^ 1 << distance) for i in range(lax.axis...  7.74 us
  transfers between devices with their start and end apart: 9, of which 3 were waited for; matrix products, arithmetic and copies ran while one was open for 3% of the time, Pallas kernels for 0%

profile of v1, /device:TPU:0, one launch (start us, length us, event | category | flops | bytes accessed | tf_op | source)
XLA Modules:
  0.0 281.1 jit_solution(2247221440257221664)
XLA Ops:
  8.0 0.0 all-reduce.2.cloned.1.call-start
  8.1 1.1 copy.20
  9.1 0.5 collective-permute-start
  11.0 2.8 collective-permute-start.1
  13.8 0.7 broadcast_select_fusion.6
  14.5 1.1 copy.18
  15.6 13.6 %all_gather.9.info.index = s32[64,512]{1,0:T(8,128)S(1)} all-gather(s32[16,512]{1,0:T(8,128)S(1)} %pad_add_fusion), channel_id=1, replica_groups=mesh['dom'=8,'shard'=4] {'shard'}, dimensions={0}, use_global_device_ids=true | all-gather | bytes 163840 | tf_op jit(solution)/shard_map/all_gather | solution.py:215
  29.3 1.6 collective-permute-start.2
  30.9 22.2 %all_gather.10.left_in = bf16[1024,400]{1,0:T(8,128)(2,1)S(1)} all-gather(bf16[256,400]{1,0:T(8,128)(2,1)S(1)} %copy.18), channel_id=1, replica_groups=mesh['dom'=8,'shard'=4] {'shard'}, dimensions={0}, use_global_device_ids=true | all-gather | bytes 1024000 | tf_op jit(solution)/shard_map/all_gather | solution.py:216
  53.1 18.6 %all_gather.11.right_in = bf16[1024,400]{1,0:T(8,128)(2,1)S(1)} all-gather(bf16[256,400]{1,0:T(8,128)(2,1)S(1)} %broadcast_select_fusion.5), channel_id=1, replica_groups=mesh['dom'=8,'shard'=4] {'shard'}, dimensions={0}, use_global_device_ids=true | all-gather | bytes 1024000 | tf_op jit(solution)/shard_map/all_gather | solution.py:218
  71.8 30.0 %bucket.1 = (bf16[1024,400]{1,0:T(8,128)(2,1)}, bf16[1024,400]{1,0:T(8,128)(2,1)}, f32[2,400,400]{2,1,0:T(8,128)}) custom-call(s32[64,512]{1,0:T(8,128)S(1)} %all_gather.9.info.index, s32[64,512]{1,0:T(8,128)S(1)} %all_gather.9.info.index, bf16[1024,400]{1,0:T(8,128)(2,1)S(1)} %all_gather.10.left_in, bf16[1024,400]{1,0:T(8,128)(2,1)S(1)} %all_gather.11.right_in, ...), custom_call_target="tpu_custom_call" | custom-call | tf_op jit(solution)/shard_map/bucket/pallas_call | solution.py:167
  101.8 0.0 reduce-scatter.5.cloned.1.call-start
  101.9 0.5 reduce-scatter.5.cloned.1.call-update
  102.4 0.0 reduce-scatter.3.cloned.1.call-start
  102.4 0.5 reduce-scatter.3.cloned.1.call-update
  103.0 146.1 %all-reduce.2.cloned.1.call-done = f32[2,400,400]{2,1,0:T(8,128)} async-done(((f32[2,400,400]{2,1,0:T(8,128)}), f32[2,400,400]{2,1,0:T(8,128)}) %all-reduce.2.cloned.1.call-update) | async-done | bytes 1280016 | tf_op jit(solution)/shard_map/psum | solution.py:227
  249.1 1.8 multiply_reduce_fusion
  250.9 0.6 fusion.8
  251.5 1.5 divide_subtract_fusion
  253.0 1.2 fusion.3
  254.1 1.0 broadcast_select_fusion
  255.1 1.4 collective-permute-start.4
  256.6 0.6 fusion.10
  257.2 6.8 %collective-permute-done.4 = bf16[256,400]{1,0:T(8,128)(2,1)S(1)} collective-permute-done((bf16[256,400]{1,0:T(8,128)(2,1)S(1)}, bf16[256,400]{1,0:T(8,128)(2,1)S(1)}, u32[]{:S(2)}, u32[]{:S(2)}) %collective-permute-start.4) | collective-permute-done | bytes 204832 | tf_op jit(solution)/shard_map/ppermute | solution.py:19
  263.9 1.4 collective-permute-start.5
  265.4 0.2 fusion.2
  265.5 0.8 copy.23
  266.4 5.6 %collective-permute-done.5 = bf16[256,400]{1,0:T(8,128)(2,1)S(1)} collective-permute-done((bf16[256,400]{1,0:T(8,128)(2,1)S(1)}, bf16[256,400]{1,0:T(8,128)(2,1)S(1)}, u32[]{:S(2)}, u32[]{:S(2)}) %collective-permute-start.5) | collective-permute-done | bytes 204832 | tf_op jit(solution)/shard_map/ppermute | solution.py:19
  271.9 0.2 fusion.7
  272.1 0.6 fusion.9
  272.7 0.2 fusion.6
  272.9 0.8 copy.24
  (36 shorter events, 0.2 us)
Async XLA Ops:
  8.0 7.6 %copy-start.5 = (s32[16,128]{1,0:T(8,128)S(1)}, s32[16,128]{1,0:T(8,128)}, u32[]{:S(2)}) copy-start(s32[16,128]{1,0:T(8,128)} %param.21) | copy-start | bytes 24580
  8.0 7.6 %copy-start.6 = (s32[16,128]{1,0:T(8,128)S(1)}, s32[16,128]{1,0:T(8,128)}, u32[]{:S(2)}) copy-start(s32[16,128]{1,0:T(8,128)} %param.20) | copy-start | bytes 24580
  8.0 7.6 %copy-start.7 = (s32[16,128]{1,0:T(8,128)S(1)}, s32[16,128]{1,0:T(8,128)}, u32[]{:S(2)}) copy-start(s32[16,128]{1,0:T(8,128)} %param.19) | copy-start | bytes 24580
  8.0 241.0 %all-reduce.2.cloned.1.call-start = ((), (), s32[]{:S(2)}) async-start(), calls=%async_computation.4 | async-start | bytes 3276800 | tf_op jit(solution)/shard_map/psum | solution.py:227
  9.1 1.8 collective-permute-start
  11.0 18.2 %collective-permute-start.1 = (bf16[256,400]{1,0:T(8,128)(2,1)S(1)}, bf16[256,400]{1,0:T(8,128)(2,1)S(1)}, u32[]{:S(2)}, u32[]{:S(2)}) collective-permute-start(bf16[256,400]{1,0:T(8,128)(2,1)S(1)} %broadcast_select_fusion.1), channel_id=1, source_target_pairs={{0,8},{4,12},{8,0},{12,4},{16,24},{20,28},{24,16},{28,20},{1,9},{5... | collective-permute-start | bytes 614408 | tf_op jit(solution)/shard_map/ppermute | solution.py:19
  15.6 56.2 %copy-start.2 = (bf16[256,400]{1,0:T(8,128)(2,1)}, bf16[256,400]{1,0:T(8,128)(2,1)S(1)}, u32[]{:S(2)}) copy-start(bf16[256,400]{1,0:T(8,128)(2,1)S(1)} %copy.18) | copy-start | bytes 614404
  29.3 23.8 %collective-permute-start.2 = (bf16[256,400]{1,0:T(8,128)(2,1)S(1)}, bf16[256,400]{1,0:T(8,128)(2,1)S(1)}, u32[]{:S(2)}, u32[]{:S(2)}) collective-permute-start(bf16[256,400]{1,0:T(8,128)(2,1)S(1)} %broadcast_select_fusion.3), channel_id=1, source_target_pairs={{0,16},{4,20},{8,24},{12,28},{16,0},{20,4},{24,8},{28,12},{1,17},{... | collective-permute-start | bytes 614408 | tf_op jit(solution)/shard_map/ppermute | solution.py:19
  101.8 149.7 %reduce-scatter.5.cloned.1.call-start = ((), (), s32[]{:S(2)}) async-start(), calls=%async_computation.3 | async-start | bytes 1310720 | tf_op jit(solution)/shard_map/reduce_scatter | solution.py:221
  101.9 149.0 %copy-start.8 = (f32[2,400]{1,0:T(2,128)S(1)}, f32[2,400]{1,0:T(2,128)}, u32[]{:S(2)}) copy-start(f32[2,400]{1,0:T(2,128)} %param.17) | copy-start | bytes 9604
  101.9 149.6 %copy-start.1 = (f32[2,400,400]{2,1,0:T(8,128)S(1)}, f32[2,400,400]{2,1,0:T(8,128)}, u32[]{:S(2)}) copy-start(f32[2,400,400]{2,1,0:T(8,128)} %oper_in.1) | copy-start | bytes 3840004
  102.4 150.6 %reduce-scatter.3.cloned.1.call-start = ((), (), s32[]{:S(2)}) async-start(), calls=%async_computation.2 | async-start | bytes 1310720 | tf_op jit(solution)/shard_map/reduce_scatter | solution.py:221
  249.1 2.4 copy-start
  251.5 2.7 collective-permute-start.3
  251.5 5.1 %copy-start.9 = (f32[256]{0:T(256)S(1)}, f32[256]{0:T(256)}, u32[]{:S(2)}) copy-start(f32[256]{0:T(256)} %param.13) | copy-start | bytes 3076
  253.0 12.4 %copy-start.3 = (bf16[256,400]{1,0:T(8,128)(2,1)S(1)}, bf16[256,400]{1,0:T(8,128)(2,1)}, u32[]{:S(2)}) copy-start(bf16[256,400]{1,0:T(8,128)(2,1)} %copy-done.2) | copy-start | bytes 614404
  253.0 12.4 %copy-start.4 = (bf16[256,400]{1,0:T(8,128)(2,1)S(1)}, bf16[256,400]{1,0:T(8,128)(2,1)}, u32[]{:S(2)}) copy-start(bf16[256,400]{1,0:T(8,128)(2,1)} %reduce-scatter.3.cloned.1.call-done) | copy-start | bytes 614404
  254.1 18.0 %copy-start.10 = (f32[256]{0:T(256)S(1)}, f32[256]{0:T(256)}, u32[]{:S(2)}) copy-start(f32[256]{0:T(256)} %param.15) | copy-start | bytes 3076
  255.1 8.8 %collective-permute-start.4 = (bf16[256,400]{1,0:T(8,128)(2,1)S(1)}, bf16[256,400]{1,0:T(8,128)(2,1)S(1)}, u32[]{:S(2)}, u32[]{:S(2)}) collective-permute-start(bf16[256,400]{1,0:T(8,128)(2,1)S(1)} %broadcast_select_fusion), channel_id=1, source_target_pairs={{0,8},{4,12},{8,0},{12,4},{16,24},{20,28},{24,16},{28,20},{1,9},{5... | collective-permute-start | bytes 614408 | tf_op jit(solution)/shard_map/ppermute | solution.py:19
  263.9 8.0 %collective-permute-start.5 = (bf16[256,400]{1,0:T(8,128)(2,1)S(1)}, bf16[256,400]{1,0:T(8,128)(2,1)S(1)}, u32[]{:S(2)}, u32[]{:S(2)}) collective-permute-start(bf16[256,400]{1,0:T(8,128)(2,1)S(1)} %broadcast_select_fusion.2), channel_id=1, source_target_pairs={{0,16},{4,20},{8,24},{12,28},{16,0},{20,4},{24,8},{28,12},{1,17},{... | collective-permute-start | bytes 614408 | tf_op jit(solution)/shard_map/ppermute | solution.py:19
Sparse Core Ops, SparseCore 0:
  101.9 147.1 all-reduce.1
Sparse Core Ops, SparseCore 1:
  104.6 25.7 reduce-scatter.4
  132.6 26.6 reduce-scatter.2

commit v2 on v1

--- a/solution.py
+++ b/solution.py
@@ -13,10 +13,7 @@
 LEARN_RATE = 0.1
 BF = jnp.bfloat16
 F32 = jnp.float32
-
-
-def from_partner(array, axis, distance):
-    return lax.ppermute(array, axis, [(i, i ^ 1 << distance) for i in range(lax.axis_size(axis))])
+MESH = pl.DeviceIdType.MESH
 
 
 def row_adagrad(weights_in, state_in, grad_in):
@@ -25,16 +22,402 @@
     return (updated, new_state)
 
 
-def level_flag(partner_bits, level_bit):
-    return jnp.bitwise_and(jnp.right_shift(partner_bits, level_bit), 1) == 1
-
-
-def move_rows(block_rows, partner_bits):
-    groups = lax.axis_size("dom")
-    for level_bit in range(groups.bit_length() - 1):
-        swapped = from_partner(block_rows, "dom", level_bit)
-        block_rows = jnp.where(level_flag(partner_bits, level_bit), swapped, block_rows)
-    return block_rows
+def flip(position, bit):
+    return position + bit - 2 * bit * ((position // bit) % 2)
+
+
+def partners(groups):
+    dom, shard = lax.axis_index("dom"), lax.axis_index("shard")
+    levels = [{"dom": flip(dom, 1 << l)} for l in range(groups.bit_length() - 1)]
+    return levels, {"shard": flip(shard, 1)}, {"shard": flip(shard, 2)}
+
+
+def is_home():
+    return lax.axis_index("dom") % 2 == lax.axis_index("shard") // 2
+
+
+def meet(others):
+    barrier = pltpu.get_barrier_semaphore()
+    for other in others:
+        pl.semaphore_signal(barrier, inc=1, device_id=other, device_id_type=MESH)
+    pl.semaphore_wait(barrier, len(others))
+
+
+def level_orders(levels):
+    order = list(range(levels))
+    return [order, order[:1] + order[1:][::-1]]
+
+
+def remote(src, dst, send_sem, recv_sem, other):
+    return pltpu.make_async_remote_copy(
+        src_ref=src,
+        dst_ref=dst,
+        send_sem=send_sem,
+        recv_sem=recv_sem,
+        device_id=other,
+        device_id_type=MESH,
+    )
+
+
+class Swaps:
+    def __init__(self, levels, mask, held, came, send_sem, recv_sem):
+        self.levels, self.mask, self.held, self.came = levels, mask, held, came
+        self.send_sem, self.recv_sem = send_sem, recv_sem
+        self.orders = level_orders(len(levels))
+
+    def copy(self, half, step):
+        return remote(
+            self.held.at[half, step],
+            self.came.at[half, step],
+            self.send_sem.at[half, step],
+            self.recv_sem.at[half, step],
+            self.levels[self.orders[half][step]],
+        )
+
+    def start(self, step):
+        for half in range(2):
+            self.copy(half, step).start()
+
+    def end(self, step):
+        for half in range(2):
+            self.copy(half, step).wait()
+            bit = 1 << self.orders[half][step]
+            flag = (self.mask[0] // bit) % 2
+            wide = jnp.full(self.held.shape[2:], flag, jnp.int32)
+            self.held[half, step + 1] = jnp.where(
+                wide == 1, self.came[half, step].astype(F32), self.held[half, step].astype(F32)
+            ).astype(BF)
+            if step + 1 < len(self.levels):
+                self.copy(half, step + 1).start()
+
+    def put(self, rows):
+        half = rows.shape[0] // 2
+        for part in range(2):
+            self.held[part, 0] = rows[part * half : (part + 1) * half].astype(BF)
+
+
+def shard_rows(ref, j, rows):
+    at = lax.axis_index("shard")
+    for bit in (1, 2):
+        if j & bit:
+            at = flip(at, bit)
+    return ref.at[pl.ds(pl.multiple_of(at * rows, rows), rows)]
+
+
+def collect_kernel(
+    groups, mask, lists, left, right, all_lists, all_left, all_right,
+    held, came, fetched, dsend, drecv, zsend, csend, recv,
+):
+    levels, near, far = partners(groups)
+    core = levels[0]
+    home = is_home()
+    away = jnp.logical_not(home)
+    sources = (lists, left, fetched)
+    totals = (all_lists, all_left, all_right)
+
+    def piece(t, j):
+        return shard_rows(totals[t], j, sources[t].shape[0])
+
+    def to_near(t, j):
+        return remote(piece(t, j), piece(t, j), zsend.at[t, j], recv.at[t, j + 1], near)
+
+    def to_core(t, j):
+        return remote(piece(t, j), piece(t, j), csend.at[t, j], recv.at[t, j], core)
+
+    def to_far(t):
+        return remote(sources[t], piece(t, 0), zsend.at[t, 0], recv.at[t, 2], far)
+
+    def begin(t):
+        @pl.when(home)
+        def _():
+            piece(t, 0)[...] = sources[t][...]
+            to_near(t, 0).start()
+            to_core(t, 0).start()
+
+        @pl.when(away)
+        def _():
+            to_far(t).start()
+
+    def relay(t):
+        @pl.when(home)
+        def _():
+            to_core(t, 2).wait_recv()
+            to_near(t, 2).start()
+            to_core(t, 2).start()
+
+    def spread(t):
+        @pl.when(home)
+        def _():
+            for j in (1, 3):
+                to_core(t, j).wait_recv()
+                to_core(t, j).start()
+
+    def finish(t):
+        @pl.when(home)
+        def _():
+            for j in (0, 2):
+                to_near(t, j).wait_send()
+            for j in range(4):
+                to_core(t, j).wait_send()
+
+        @pl.when(away)
+        def _():
+            to_far(t).wait_send()
+            for j in range(4):
+                to_core(t, j).wait_recv()
+
+    swaps = Swaps(levels, mask, held, came, dsend, drecv)
+    swaps.put(right)
+    meet(levels + [near, far])
+    swaps.start(0)
+    begin(0)
+    begin(1)
+    for step in range(len(levels)):
+        swaps.end(step)
+        if step == 0:
+            relay(0)
+        if step == min(1, len(levels) - 1):
+            relay(1)
+    half = fetched.shape[0] // 2
+    for part in range(2):
+        fetched[part * half : (part + 1) * half, :] = held[part, len(levels)]
+    begin(2)
+    spread(0)
+    spread(1)
+    relay(2)
+    spread(2)
+    for t in range(3):
+        finish(t)
+
+
+def collect(mask, lists, left, right):
+    groups, shards = lax.axis_size("dom"), lax.axis_size("shard")
+    rows, width = left.shape
+    steps = groups.bit_length() - 1
+    vmem = pl.BlockSpec(memory_space=pltpu.VMEM)
+    dma = pltpu.SemaphoreType.DMA
+    return pl.pallas_call(
+        functools.partial(collect_kernel, groups),
+        in_specs=[pl.BlockSpec(memory_space=pltpu.SMEM)] + [vmem] * 3,
+        out_specs=[vmem] * 3,
+        out_shape=[
+            jax.ShapeDtypeStruct((shards * lists.shape[0], lists.shape[1]), lists.dtype),
+            jax.ShapeDtypeStruct((shards * rows, width), BF),
+            jax.ShapeDtypeStruct((shards * rows, width), BF),
+        ],
+        scratch_shapes=[
+            pltpu.VMEM((2, steps + 1, rows // 2, width), BF),
+            pltpu.VMEM((2, steps, rows // 2, width), BF),
+            pltpu.VMEM((rows, width), BF),
+            dma((2, steps)),
+            dma((2, steps)),
+            dma((3, 4)),
+            dma((3, 4)),
+            dma((3, 4)),
+        ],
+        compiler_params=pltpu.CompilerParams(
+            collective_id=0, has_side_effects=True, vmem_limit_bytes=32 * 1024 * 1024
+        ),
+        name="collect",
+    )(mask, lists, left, right)
+
+
+def reduce_kernel(
+    groups, mask, right, left, oper, own_right, own_left, oper_total,
+    held, came, core_in, near_in, far_in, out_going, own_sum, piece_in, work,
+    dsend, drecv, csend, crecv, nsend, nrecv, fsend, frecv, osend, orecv, gsend, grecv,
+):
+    levels, near, far = partners(groups)
+    core = levels[0]
+    home = is_home()
+    away = jnp.logical_not(home)
+    totals = (right, left)
+    rows = own_right.shape[0]
+    dom, shard = lax.axis_index("dom"), lax.axis_index("shard")
+
+    def to_core(t, j):
+        return remote(
+            shard_rows(totals[t], j, rows), core_in.at[t, j], csend.at[t, j], crecv.at[t, j], core
+        )
+
+    def to_near(t, j):
+        return remote(
+            out_going.at[t, j], near_in.at[t, j // 2], nsend.at[t, j // 2], nrecv.at[t, j // 2], near
+        )
+
+    def to_far(t):
+        return remote(out_going.at[t, 2], far_in.at[t], fsend.at[t], frecv.at[t], far)
+
+    def begin(t):
+        @pl.when(away)
+        def _():
+            for j in (1, 3, 0, 2):
+                to_core(t, j).start()
+
+    def pair_sum(t, j):
+        return shard_rows(totals[t], j, rows)[...].astype(F32) + core_in[t, j].astype(F32)
+
+    def first(t):
+        @pl.when(home)
+        def _():
+            for j in (1, 3):
+                to_core(t, j).wait_recv()
+                out_going[t, j] = pair_sum(t, j).astype(BF)
+                to_near(t, j).start()
+
+    def second(t):
+        @pl.when(home)
+        def _():
+            for j in (2, 0):
+                to_core(t, j).wait_recv()
+                to_near(t, j).wait_recv()
+                total = pair_sum(t, j) + near_in[t, j // 2].astype(F32)
+                if j == 2:
+                    out_going[t, 2] = total.astype(BF)
+                    to_far(t).start()
+                else:
+                    own_sum[t] = total
+
+    def third(t):
+        @pl.when(away)
+        def _():
+            to_far(t).wait_recv()
+            own_sum[t] = far_in[t].astype(F32)
+
+    def finish(t):
+        @pl.when(home)
+        def _():
+            for j in (1, 3):
+                to_near(t, j).wait_send()
+            to_far(t).wait_send()
+
+        @pl.when(away)
+        def _():
+            for j in range(4):
+                to_core(t, j).wait_send()
+
+    every = levels + [near, far]
+    bits = [(dom // (1 << l)) % 2 for l in range(len(levels))] + [shard % 2, (shard // 2) % 2]
+    spans, starts = [oper.shape[0]], [jnp.int32(0) + shard * 0]
+    for l in range(len(every)):
+        if spans[-1] >= 32:
+            spans.append(spans[-1] // 2)
+            starts.append(starts[-1] + bits[l] * spans[-1])
+        else:
+            spans.append(spans[-1])
+            starts.append(starts[-1])
+    lands = [0]
+    for l in range(len(every)):
+        lands.append(lands[-1] + spans[l + 1])
+
+    def window(ref, start, span):
+        return ref.at[pl.ds(pl.multiple_of(start, 16), span)]
+
+    def oper_copy(l):
+        span = spans[l + 1]
+        start = starts[l] + (1 - bits[l]) * span if span < spans[l] else starts[l]
+        return remote(
+            window(work, start, span), piece_in.at[pl.ds(lands[l], span)], osend.at[l], orecv.at[l], every[l]
+        )
+
+    def oper_end(l):
+        oper_copy(l).wait()
+        span = spans[l + 1]
+        at = pl.ds(pl.multiple_of(starts[l + 1], 16), span)
+        total = work[at, :].astype(F32) + piece_in[pl.ds(lands[l], span), :].astype(F32)
+        work[at, :] = total.astype(BF)
+
+    halved = [l for l in range(len(every)) if spans[l + 1] < spans[l]]
+
+    def back_copy(l):
+        part = window(oper_total, starts[l + 1], spans[l + 1])
+        return remote(part, part, gsend.at[l], grecv.at[l], every[l])
+
+    swaps = Swaps(levels, mask, held, came, dsend, drecv)
+    work[...] = oper[...].astype(BF)
+    meet(every)
+    begin(0)
+    oper_copy(0).start()
+    begin(1)
+    last = len(every)
+    todo = {
+        0: lambda: (first(0), first(1)),
+        1: lambda: second(0),
+        2: lambda: (third(0), swaps.put(own_sum.at[0]), swaps.start(0), second(1)),
+    }
+    for l in range(last):
+        if l in todo:
+            todo[l]()
+        if l >= 3 and l - 3 < len(levels):
+            swaps.end(l - 3)
+        oper_end(l)
+        if l + 1 < last:
+            oper_copy(l + 1).start()
+    window(oper_total, starts[-1], spans[-1])[...] = window(work, starts[-1], spans[-1])[...]
+    backs = halved[::-1]
+    step = last - 3
+    for l in backs:
+        back_copy(l).start()
+        if step < len(levels):
+            swaps.end(step)
+            step += 1
+        back_copy(l).wait()
+    for rest in range(step, len(levels)):
+        swaps.end(rest)
+    half = rows // 2
+    for part in range(2):
+        own_right[part * half : (part + 1) * half, :] = held[part, len(levels)]
+    third(1)
+    own_left[...] = own_sum[1]
+    for t in range(2):
+        finish(t)
+
+
+def reduce(mask, grad_right, grad_left, grad_oper):
+    groups, shards = lax.axis_size("dom"), lax.axis_size("shard")
+    part, width = grad_left.shape
+    rows = part // shards
+    steps = groups.bit_length() - 1
+    every = steps + 2
+    vmem = pl.BlockSpec(memory_space=pltpu.VMEM)
+    dma = pltpu.SemaphoreType.DMA
+    return pl.pallas_call(
+        functools.partial(reduce_kernel, groups),
+        in_specs=[pl.BlockSpec(memory_space=pltpu.SMEM)] + [vmem] * 3,
+        out_specs=[vmem] * 3,
+        out_shape=[
+            jax.ShapeDtypeStruct((rows, width), BF),
+            jax.ShapeDtypeStruct((rows, width), F32),
+            jax.ShapeDtypeStruct(grad_oper.shape, BF),
+        ],
+        scratch_shapes=[
+            pltpu.VMEM((2, steps + 1, rows // 2, width), BF),
+            pltpu.VMEM((2, steps, rows // 2, width), BF),
+            pltpu.VMEM((2, 4, rows, width), BF),
+            pltpu.VMEM((2, 2, rows, width), BF),
+            pltpu.VMEM((2, rows, width), BF),
+            pltpu.VMEM((2, 4, rows, width), BF),
+            pltpu.VMEM((2, rows, width), F32),
+            pltpu.VMEM((grad_oper.shape[0] + 16 * every, width), BF),
+            pltpu.VMEM(grad_oper.shape, BF),
+            dma((2, steps)),
+            dma((2, steps)),
+            dma((2, 4)),
+            dma((2, 4)),
+            dma((2, 2)),
+            dma((2, 2)),
+            dma((2,)),
+            dma((2,)),
+            dma((every,)),
+            dma((every,)),
+            dma((every,)),
+            dma((every,)),
+        ],
+        compiler_params=pltpu.CompilerParams(
+            collective_id=1, has_side_effects=True, vmem_limit_bytes=40 * 1024 * 1024
+        ),
+        name="reduce",
+    )(mask, grad_right, grad_left, grad_oper)
 
 
 def dot(a, b, dims):
@@ -84,7 +467,7 @@
     right_sum,
     oper_sum,
 ):
-    me = lax.axis_index("shard")
+    me = (lax.axis_index("shard") % 2) * 2 + lax.axis_index("dom") % 2
     for wide, narrow in ((left, left_in), (right, right_in)):
         wide[:, 384:] = jnp.zeros((wide.shape[0], WIDE - 384), BF)
         wide[:, :D] = narrow[...]
@@ -155,7 +538,8 @@
     lax.fori_loop(0, (mine + 1) // 2, visit, 0)
     left_out[...] = left_sum[:, :D].astype(BF)
     right_out[...] = right_sum[:, :D].astype(BF)
-    oper_out[...] = oper_sum[:, :D, :D]
+    for relation in range(oper_sum.shape[0]):
+        oper_out[relation * WIDE : (relation + 1) * WIDE, :] = oper_sum[relation, :, :D]
 
 
 def bucket(packed, left_part, right_part, operators):
@@ -174,11 +558,11 @@
             whole(right_part.shape),
             whole(operators.shape),
         ],
-        out_specs=[whole((part, D)), whole((part, D)), whole(operators.shape)],
+        out_specs=[whole((part, D)), whole((part, D)), whole((nrel * WIDE, D))],
         out_shape=[
             jax.ShapeDtypeStruct((part, D), BF),
             jax.ShapeDtypeStruct((part, D), BF),
-            jax.ShapeDtypeStruct(operators.shape, F32),
+            jax.ShapeDtypeStruct((nrel * WIDE, D), F32),
         ],
         scratch_shapes=[
             pltpu.VMEM((part, WIDE), BF),
@@ -207,24 +591,16 @@
     block_relation,
     edge_count,
 ):
-    partner_bits = partner_mask[0]
     blocks = block_relation.shape[0]
     lane = lax.broadcasted_iota(jnp.int32, (blocks, 128), 1)
     info = jnp.where(lane == 0, block_relation[:, None], edge_count[0])
     packed = jnp.concatenate([edge_lhs, edge_rhs, negatives, info], axis=1)
-    packed = lax.all_gather(packed, "shard", axis=0, tiled=True)
-    left_part = lax.all_gather(lhs_emb, "shard", axis=0, tiled=True)
-    fetched = move_rows(rhs_emb, partner_bits)
-    right_part = lax.all_gather(fetched, "shard", axis=0, tiled=True)
-    grad_left, grad_right, grad_oper = bucket(packed, left_part, right_part, operators)
-    own_left, own_right = (
-        lax.psum_scatter(g, "shard", scatter_dimension=0, tiled=True)
-        for g in (grad_left, grad_right)
-    )
-    owner_right = move_rows(own_right, partner_bits)
-    new_lhs, new_lhs_acc = row_adagrad(lhs_emb, lhs_acc, own_left.astype(F32))
-    new_rhs, new_rhs_acc = row_adagrad(rhs_emb, rhs_acc, owner_right.astype(F32))
-    total_oper = lax.psum(grad_oper, ("dom", "shard"))
+    lists, left_part, right_part = collect(partner_mask, packed, lhs_emb, rhs_emb)
+    grad_left, grad_right, grad_oper = bucket(lists, left_part, right_part, operators)
+    own_right, own_left, total_oper = reduce(partner_mask, grad_right, grad_left, grad_oper)
+    new_lhs, new_lhs_acc = row_adagrad(lhs_emb, lhs_acc, own_left)
+    new_rhs, new_rhs_acc = row_adagrad(rhs_emb, rhs_acc, own_right.astype(F32))
+    total_oper = total_oper.reshape(operators.shape[0], WIDE, D)[:, :D].astype(F32)
     new_operators, new_operator_acc = row_adagrad(operators, operator_acc, total_oper)
     return (
         new_lhs.astype(BF),

time: 280 us -> 115 us (0.41); the launches traced: 281 us -> 113 us
  waiting for transfers between devices: 159 us -> 0 us
  Pallas kernels: 30 us -> 97 us
  blocking collectives: 54.5 us -> 0 us
  between operations: 17 us -> 2 us
  starting transfers between devices: 7.86 us -> 0 us
  local copies, waits for them, and re-layouts: 3.82 us -> 7.75 us
    psum x1 -> x0, waiting for transfers between devices: 146 us -> none  [per_device(): total_oper = lax.psum(grad_oper, ('dom', 'shard'))]
    pallas_call x0 -> x2, Pallas kernels: none -> 79 us  [the longest x1 48.6 us: reduce(): pl.pallas_call(functools.partial(reduce_kernel, groups), in_specs=[pl.Blo...]
    all_gather x3 -> x0, blocking collectives: 54.5 us -> none  [the longest x1 22.2 us: per_device(): left_part = lax.all_gather(lhs_emb, 'shard', axis=0, tiled=True)]
    ppermute x6 -> x0, waiting for transfers between devices: 12.3 us -> none  [from_partner(): lax.ppermute(array, axis, [(i, i ^ 1 << distance) for i in range(lax.axis...]
    pallas_call x1, Pallas kernels: 30 us -> 18 us  [bucket(): pl.pallas_call(functools.partial(bucket_kernel, groups, total // groups),...]
    ppermute x6 -> x0, starting transfers between devices: 7.74 us -> none  [from_partner(): lax.ppermute(array, axis, [(i, i ^ 1 << distance) for i in range(lax.axis...]
    unnamed x26 -> x16, local copies, waits for them, and re-layouts: 3.82 us -> 7.75 us
  transfers between devices with their start and end apart: 9 -> 0, of which waited for: 3 -> 0; matrix products, arithmetic and copies ran while one was open for 3% -> 0% of each run, Pallas kernels for 0% -> 0%
where the time goes in v2:
time: 115 us; the launch traced here: 113 us
  Pallas kernels  97 us (84%)
  local copies, waits for them, and re-layouts  7.75 us (7%)
  other arithmetic  6.06 us (5%)
  between operations  2 us (2%)
    pallas_call x1, Pallas kernels, reduce(): pl.pallas_call(functools.partial(reduce_kernel, groups), in_specs=[pl.Blo...  48.6 us
    pallas_call x1, Pallas kernels, collect(): pl.pallas_call(functools.partial(collect_kernel, groups), in_specs=[pl.Bl...  30.4 us
    pallas_call x1, Pallas kernels, bucket(): pl.pallas_call(functools.partial(bucket_kernel, groups, total // groups),...  18 us
    unnamed x16, local copies, waits for them, and re-layouts  7.75 us

profile of v2, /device:TPU:0, one launch (start us, length us, event | category | flops | bytes accessed | tf_op | source)
XLA Modules:
  0.0 112.8 jit_solution(3684483077390158350)
XLA Ops:
  1.9 0.7 broadcast_select_fusion
  2.7 0.7 pad_add_fusion.lists
  3.4 1.1 copy.18.left
  4.5 1.1 copy.20.right
  5.5 30.4 %collect.1 = (s32[64,512]{1,0:T(8,128)S(1)}, bf16[1024,400]{1,0:T(8,128)(2,1)S(1)}, bf16[1024,400]{1,0:T(8,128)(2,1)S(1)}) custom-call(s32[1]{0:T(128)S(6)} %copy.24.mask, s32[16,512]{1,0:T(8,128)S(1)} %pad_add_fusion.lists, bf16[256,400]{1,0:T(8,128)(2,1)S(1)} %copy.18.left, bf16[256,400]{1,0:T(8,128)(2,1)S(1)} %copy.20.right), custom_call_target="tpu_custom_call" | custom-call | tf_op jit(solution)/shard_map/collect/pallas_call | solution.py:199
  35.9 0.0 copy-start
  35.9 1.4 %copy-done = f32[2,400,400]{2,1,0:T(8,128)S(1)} copy-done((f32[2,400,400]{2,1,0:T(8,128)S(1)}, f32[2,400,400]{2,1,0:T(8,128)}, u32[]{:S(2)}) %copy-start) | copy-done | bytes 1280024
  37.4 18.0 %bucket.1 = (bf16[1024,400]{1,0:T(8,128)(2,1)S(1)}, bf16[1024,400]{1,0:T(8,128)(2,1)S(1)}, f32[1024,400]{1,0:T(8,128)}) custom-call(s32[64,512]{1,0:T(8,128)S(1)} %get-tuple-element.15.info.index, s32[64,512]{1,0:T(8,128)S(1)} %get-tuple-element.15.info.index, bf16[1024,400]{1,0:T(8,128)(2,1)S(1)} %get-tuple-element.16.left_in, ...), custom_call_target="tpu_custom_call" | custom-call | tf_op jit(solution)/shard_map/bucket/pallas_call | solution.py:551
  55.4 0.0 copy-start.2
  55.4 1.6 %copy-done.2 = f32[1024,400]{1,0:T(8,128)S(1)} copy-done((f32[1024,400]{1,0:T(8,128)S(1)}, f32[1024,400]{1,0:T(8,128)}, u32[]{:S(2)}) %copy-start.2) | copy-done | bytes 1638424
  57.0 0.0 copy-start.4
  57.0 0.0 copy-start.5
  57.0 48.6 %reduce.1 = (bf16[256,400]{1,0:T(8,128)(2,1)S(1)}, f32[256,400]{1,0:T(8,128)S(1)}, bf16[1024,400]{1,0:T(8,128)(2,1)S(1)}) custom-call(s32[1]{0:T(128)S(6)} %copy.24.mask, bf16[1024,400]{1,0:T(8,128)(2,1)S(1)} %get-tuple-element.18.right, bf16[1024,400]{1,0:T(8,128)(2,1)S(1)} %get-tuple-element.19.left, f32[1024,400]{1,0:T(8,128)S(1)} %copy-done.2), custom_call_target="tpu_custom_call" | custom-call | tf_op jit(solution)/shard_map/reduce/pallas_call | solution.py:384
  105.6 0.1 multiply_reduce_fusion
  105.7 0.1 fusion.6
  105.9 0.0 copy-done.4
  105.9 0.0 copy-start.3
  105.9 0.6 fusion.8
  106.5 0.0 copy-done.5
  106.5 0.6 fusion.9
  107.0 0.0 copy-start.1
  107.0 0.9 fusion.5
  107.9 1.8 %copy.23 = bf16[256,400]{0,1:T(8,128)(2,1)} copy(bf16[256,400]{1,0:T(8,128)(2,1)} %get-tuple-element.36) | data formatting | bytes 409600
  109.7 0.3 fusion.2
  110.0 0.0 copy-done.3
  110.0 0.6 fusion.7
  110.6 0.8 copy.22
  111.4 0.0 copy-done.1
  111.4 1.4 %fusion.1 = f32[2,400,400]{2,1,0:T(8,128)} fusion(f32[2,400,400]{2,1,0:T(8,128)S(1)} %copy-done.1, f32[2,400]{1,0:T(2,128)S(1)} %get-tuple-element.30, bf16[2,512,400]{2,1,0:T(8,128)(2,1)S(1)} %bitcast.4), kind=kLoop, calls=%fused_computation.3 | loop fusion | flops 1280000 | bytes 3203200 | tf_op jit(solution)/shard_map/sub | solution.py:21
  (1 shorter events, 0.0 us)
Async XLA Ops:
  35.9 1.4 %copy-start = (f32[2,400,400]{2,1,0:T(8,128)S(1)}, f32[2,400,400]{2,1,0:T(8,128)}, u32[]{:S(2)}) copy-start(f32[2,400,400]{2,1,0:T(8,128)} %oper_in.1) | copy-start | bytes 3840004
  55.4 1.6 %copy-start.2 = (f32[1024,400]{1,0:T(8,128)S(1)}, f32[1024,400]{1,0:T(8,128)}, u32[]{:S(2)}) copy-start(f32[1024,400]{1,0:T(8,128)} %get-tuple-element.20.oper) | copy-start | bytes 4915204
  57.0 48.9 %copy-start.4 = (f32[256]{0:T(256)S(1)}, f32[256]{0:T(256)}, u32[]{:S(2)}) copy-start(f32[256]{0:T(256)} %param.15) | copy-start | bytes 3076
  57.0 49.5 %copy-start.5 = (f32[256]{0:T(256)S(1)}, f32[256]{0:T(256)}, u32[]{:S(2)}) copy-start(f32[256]{0:T(256)} %param.13) | copy-start | bytes 3076
  105.9 4.1 %copy-start.3 = (f32[2,400]{1,0:T(2,128)S(1)}, f32[2,400]{1,0:T(2,128)}, u32[]{:S(2)}) copy-start(f32[2,400]{1,0:T(2,128)} %param.17) | copy-start | bytes 9604
  107.0 4.4 %copy-start.1 = (f32[2,400,400]{2,1,0:T(8,128)S(1)}, f32[2,400,400]{2,1,0:T(8,128)}, u32[]{:S(2)}) copy-start(f32[2,400,400]{2,1,0:T(8,128)} %oper_in.1) | copy-start | bytes 3840004

commit v3 on v2

--- a/solution.py
+++ b/solution.py
@@ -9,17 +9,13 @@
 
 D = 400
 WIDE = 512
+MAIN = 384
+REST = D - MAIN
 SPAN = 128
 LEARN_RATE = 0.1
 BF = jnp.bfloat16
 F32 = jnp.float32
 MESH = pl.DeviceIdType.MESH
-
-
-def row_adagrad(weights_in, state_in, grad_in):
-    new_state = state_in + jnp.mean(grad_in * grad_in, axis=-1)
-    updated = weights_in.astype(F32) - LEARN_RATE * grad_in / jnp.sqrt(new_state)[..., None]
-    return (updated, new_state)
 
 
 def flip(position, bit):
@@ -57,6 +53,16 @@
         device_id=other,
         device_id_type=MESH,
     )
+
+
+def packed_rows(rows):
+    return rows + REST
+
+
+def pack(main, rest):
+    turned = jnp.transpose(rest)[:REST, :].astype(BF)
+    blank = jnp.zeros((REST, MAIN - turned.shape[1]), BF)
+    return main.astype(BF), jnp.concatenate([turned, blank], axis=1)
 
 
 class Swaps:
@@ -106,13 +112,14 @@
 
 def collect_kernel(
     groups, mask, lists, left, right, all_lists, all_left, all_right,
-    held, came, fetched, dsend, drecv, zsend, csend, recv,
+    held, came, fetched, mine, rest, dsend, drecv, zsend, csend, recv,
 ):
     levels, near, far = partners(groups)
     core = levels[0]
     home = is_home()
     away = jnp.logical_not(home)
-    sources = (lists, left, fetched)
+    sources = (lists, mine, fetched)
+    rows = left.shape[0]
     totals = (all_lists, all_left, all_right)
 
     def piece(t, j):
@@ -167,7 +174,11 @@
                 to_core(t, j).wait_recv()
 
     swaps = Swaps(levels, mask, held, came, dsend, drecv)
-    swaps.put(right)
+    for raw, whole in ((right, fetched), (left, mine)):
+        rest[...] = jnp.zeros_like(rest)
+        rest[:, :REST] = raw[:, MAIN:].astype(F32)
+        whole[:rows, :], whole[rows:, :] = pack(raw[:, :MAIN], rest[...])
+    swaps.put(fetched)
     meet(levels + [near, far])
     swaps.start(0)
     begin(0)
@@ -192,7 +203,7 @@
 
 def collect(mask, lists, left, right):
     groups, shards = lax.axis_size("dom"), lax.axis_size("shard")
-    rows, width = left.shape
+    rows, width = packed_rows(left.shape[0]), MAIN
     steps = groups.bit_length() - 1
     vmem = pl.BlockSpec(memory_space=pltpu.VMEM)
     dma = pltpu.SemaphoreType.DMA
@@ -209,6 +220,8 @@
             pltpu.VMEM((2, steps + 1, rows // 2, width), BF),
             pltpu.VMEM((2, steps, rows // 2, width), BF),
             pltpu.VMEM((rows, width), BF),
+            pltpu.VMEM((rows, width), BF),
+            pltpu.VMEM((left.shape[0], 128), F32),
             dma((2, steps)),
             dma((2, steps)),
             dma((3, 4)),
@@ -224,7 +237,7 @@
 
 def reduce_kernel(
     groups, mask, right, left, oper, own_right, own_left, oper_total,
-    held, came, core_in, near_in, far_in, out_going, own_sum, piece_in, work,
+    held, came, core_in, near_in, far_in, out_going, own_sum, piece_in, leaving, work,
     dsend, drecv, csend, crecv, nsend, nrecv, fsend, frecv, osend, orecv, gsend, grecv,
 ):
     levels, near, far = partners(groups)
@@ -298,71 +311,90 @@
 
     every = levels + [near, far]
     bits = [(dom // (1 << l)) % 2 for l in range(len(levels))] + [shard % 2, (shard // 2) % 2]
-    spans, starts = [oper.shape[0]], [jnp.int32(0) + shard * 0]
-    for l in range(len(every)):
-        if spans[-1] >= 32:
-            spans.append(spans[-1] // 2)
-            starts.append(starts[-1] + bits[l] * spans[-1])
-        else:
-            spans.append(spans[-1])
-            starts.append(starts[-1])
-    lands = [0]
-    for l in range(len(every)):
-        lands.append(lands[-1] + spans[l + 1])
-
-    def window(ref, start, span):
-        return ref.at[pl.ds(pl.multiple_of(start, 16), span)]
-
-    def oper_copy(l):
-        span = spans[l + 1]
-        start = starts[l] + (1 - bits[l]) * span if span < spans[l] else starts[l]
+    last = len(every)
+    tail = list(range(len(levels), last))
+    chains = [order + tail for order in level_orders(len(levels))]
+    nrel = work.shape[0]
+    spans, lands = [work.shape[1]], [0]
+    for step in range(last):
+        spans.append(spans[-1] // 2 if spans[-1] >= 32 else spans[-1])
+        lands.append(lands[-1] + spans[-1])
+    starts = []
+    for r in range(nrel):
+        at = [shard * 0]
+        for step in range(last):
+            halves = spans[step + 1] < spans[step]
+            at.append(at[-1] + bits[chains[r % 2][step]] * spans[step + 1] if halves else at[-1])
+        starts.append(at)
+
+    def window(ref, r, start, span):
+        return ref.at[r, pl.ds(pl.multiple_of(start, 16), span)]
+
+    def oper_copy(r, step):
+        land = pl.ds(lands[step], spans[step + 1])
         return remote(
-            window(work, start, span), piece_in.at[pl.ds(lands[l], span)], osend.at[l], orecv.at[l], every[l]
+            leaving.at[r, land],
+            piece_in.at[r, land],
+            osend.at[r, step],
+            orecv.at[r, step],
+            every[chains[r % 2][step]],
         )
 
-    def oper_end(l):
-        oper_copy(l).wait()
-        span = spans[l + 1]
-        at = pl.ds(pl.multiple_of(starts[l + 1], 16), span)
-        total = work[at, :].astype(F32) + piece_in[pl.ds(lands[l], span), :].astype(F32)
-        work[at, :] = total.astype(BF)
-
-    halved = [l for l in range(len(every)) if spans[l + 1] < spans[l]]
-
-    def back_copy(l):
-        part = window(oper_total, starts[l + 1], spans[l + 1])
-        return remote(part, part, gsend.at[l], grecv.at[l], every[l])
+    def oper_start(step):
+        for r in range(nrel):
+            span, start = spans[step + 1], starts[r][step]
+            if span < spans[step]:
+                start = start + (1 - bits[chains[r % 2][step]]) * span
+            leaving[r, pl.ds(lands[step], span)] = window(work, r, start, span)[...].astype(BF)
+            oper_copy(r, step).start()
+
+    def oper_end(step):
+        for r in range(nrel):
+            oper_copy(r, step).wait()
+            span = spans[step + 1]
+            land = pl.ds(lands[step], span)
+            own = window(work, r, starts[r][step + 1], span)
+            kept = own[...] if span < spans[step] else leaving[r, land].astype(F32)
+            own[...] = kept + piece_in[r, land].astype(F32)
+
+    def back_copy(r, step):
+        part = window(oper_total, r, starts[r][step + 1], spans[step + 1])
+        return remote(part, part, gsend.at[r, step], grecv.at[r, step], every[chains[r % 2][step]])
 
     swaps = Swaps(levels, mask, held, came, dsend, drecv)
-    work[...] = oper[...].astype(BF)
+    work[...] = oper[...]
     meet(every)
     begin(0)
-    oper_copy(0).start()
+    oper_start(0)
     begin(1)
-    last = len(every)
     todo = {
         0: lambda: (first(0), first(1)),
         1: lambda: second(0),
         2: lambda: (third(0), swaps.put(own_sum.at[0]), swaps.start(0), second(1)),
     }
-    for l in range(last):
-        if l in todo:
-            todo[l]()
-        if l >= 3 and l - 3 < len(levels):
-            swaps.end(l - 3)
-        oper_end(l)
-        if l + 1 < last:
-            oper_copy(l + 1).start()
-    window(oper_total, starts[-1], spans[-1])[...] = window(work, starts[-1], spans[-1])[...]
-    backs = halved[::-1]
-    step = last - 3
-    for l in backs:
-        back_copy(l).start()
-        if step < len(levels):
-            swaps.end(step)
-            step += 1
-        back_copy(l).wait()
-    for rest in range(step, len(levels)):
+    for step in range(last):
+        if step in todo:
+            todo[step]()
+        if 3 <= step < 3 + len(levels):
+            swaps.end(step - 3)
+        oper_end(step)
+        if step + 1 < last:
+            oper_start(step + 1)
+    for r in range(nrel):
+        final = window(work, r, starts[r][-1], spans[-1])[...]
+        window(oper_total, r, starts[r][-1], spans[-1])[...] = final.astype(BF)
+    swap = last - 3
+    for step in reversed(range(last)):
+        if spans[step + 1] == spans[step]:
+            continue
+        for r in range(nrel):
+            back_copy(r, step).start()
+        if swap < len(levels):
+            swaps.end(swap)
+            swap += 1
+        for r in range(nrel):
+            back_copy(r, step).wait()
+    for rest in range(swap, len(levels)):
         swaps.end(rest)
     half = rows // 2
     for part in range(2):
@@ -379,6 +411,7 @@
     rows = part // shards
     steps = groups.bit_length() - 1
     every = steps + 2
+    nrel = grad_oper.shape[0]
     vmem = pl.BlockSpec(memory_space=pltpu.VMEM)
     dma = pltpu.SemaphoreType.DMA
     return pl.pallas_call(
@@ -398,8 +431,9 @@
             pltpu.VMEM((2, rows, width), BF),
             pltpu.VMEM((2, 4, rows, width), BF),
             pltpu.VMEM((2, rows, width), F32),
-            pltpu.VMEM((grad_oper.shape[0] + 16 * every, width), BF),
-            pltpu.VMEM(grad_oper.shape, BF),
+            pltpu.VMEM((nrel, grad_oper.shape[1] + 16 * every, width), BF),
+            pltpu.VMEM((nrel, grad_oper.shape[1] + 16 * every, width), BF),
+            pltpu.VMEM(grad_oper.shape, F32),
             dma((2, steps)),
             dma((2, steps)),
             dma((2, 4)),
@@ -408,10 +442,10 @@
             dma((2, 2)),
             dma((2,)),
             dma((2,)),
-            dma((every,)),
-            dma((every,)),
-            dma((every,)),
-            dma((every,)),
+            dma((nrel, every)),
+            dma((nrel, every)),
+            dma((nrel, every)),
+            dma((nrel, every)),
         ],
         compiler_params=pltpu.CompilerParams(
             collective_id=1, has_side_effects=True, vmem_limit_bytes=40 * 1024 * 1024
@@ -466,11 +500,17 @@
     left_sum,
     right_sum,
     oper_sum,
+    turn,
 ):
     me = (lax.axis_index("shard") % 2) * 2 + lax.axis_index("dom") % 2
-    for wide, narrow in ((left, left_in), (right, right_in)):
-        wide[:, 384:] = jnp.zeros((wide.shape[0], WIDE - 384), BF)
-        wide[:, :D] = narrow[...]
+    rows = left.shape[0] // groups
+    packs = packed_rows(rows)
+    for wide, packed in ((left, left_in), (right, right_in)):
+        turn[...] = jnp.zeros_like(turn)
+        for g in range(groups):
+            wide[g * rows : (g + 1) * rows, :MAIN] = packed[g * packs : g * packs + rows, :]
+            turn[:REST, :rows] = packed[g * packs + rows : (g + 1) * packs, :rows].astype(F32)
+            wide[g * rows : (g + 1) * rows, MAIN:] = jnp.transpose(turn[:, :rows]).astype(BF)
     oper[...] = jnp.zeros_like(oper)
     oper[:, :D, :D] = oper_in[...].astype(BF)
     left_sum[...] = jnp.zeros_like(left_sum)
@@ -536,16 +576,24 @@
         return carry
 
     lax.fori_loop(0, (mine + 1) // 2, visit, 0)
-    left_out[...] = left_sum[:, :D].astype(BF)
-    right_out[...] = right_sum[:, :D].astype(BF)
+    for total, out in ((left_sum, left_out), (right_sum, right_out)):
+        for g in range(groups):
+            part = total.at[g * rows : (g + 1) * rows]
+            at = g * packs
+            out[at : at + rows, :], out[at + rows : at + packs, :] = pack(part[:, :MAIN], part[:, MAIN:])
     for relation in range(oper_sum.shape[0]):
-        oper_out[relation * WIDE : (relation + 1) * WIDE, :] = oper_sum[relation, :, :D]
+        turned = jnp.transpose(oper_sum[relation, :, MAIN:])
+        oper_out[relation, :D, :] = oper_sum[relation, :D, :MAIN]
+        oper_out[relation, D:, :] = jnp.zeros((WIDE - D, MAIN), F32)
+        oper_out[relation, D : D + REST, :] = turned[:REST, :MAIN]
+        oper_out[relation, D + REST : D + 2 * REST, :128] = turned[:REST, MAIN:]
 
 
 def bucket(packed, left_part, right_part, operators):
     groups = lax.axis_size("shard")
     total, _ = packed.shape
-    part = left_part.shape[0]
+    packs = left_part.shape[0]
+    part = packs - groups * REST
     whole = lambda shape: pl.BlockSpec(shape, lambda i: (0,) * len(shape))
     nrel = operators.shape[0]
     return pl.pallas_call(
@@ -558,11 +606,11 @@
             whole(right_part.shape),
             whole(operators.shape),
         ],
-        out_specs=[whole((part, D)), whole((part, D)), whole((nrel * WIDE, D))],
+        out_specs=[whole((packs, MAIN)), whole((packs, MAIN)), whole((nrel, WIDE, MAIN))],
         out_shape=[
-            jax.ShapeDtypeStruct((part, D), BF),
-            jax.ShapeDtypeStruct((part, D), BF),
-            jax.ShapeDtypeStruct((nrel * WIDE, D), F32),
+            jax.ShapeDtypeStruct((packs, MAIN), BF),
+            jax.ShapeDtypeStruct((packs, MAIN), BF),
+            jax.ShapeDtypeStruct((nrel, WIDE, MAIN), F32),
         ],
         scratch_shapes=[
             pltpu.VMEM((part, WIDE), BF),
@@ -571,10 +619,66 @@
             pltpu.VMEM((part, WIDE), F32),
             pltpu.VMEM((part, WIDE), F32),
             pltpu.VMEM((nrel, WIDE, WIDE), F32),
+            pltpu.VMEM((128, WIDE), F32),
         ],
         compiler_params=pltpu.CompilerParams(vmem_limit_bytes=48 * 1024 * 1024),
         name="bucket",
     )(packed, packed, left_part, right_part, operators)
+
+
+def update_kernel(
+    lhs, lhs_acc, lhs_grad, rhs, rhs_acc, rhs_grad, operators, operator_acc, oper_grad,
+    new_lhs, new_lhs_acc, new_rhs, new_rhs_acc, new_operators, new_operator_acc, turn, states,
+):
+    def squares(block):
+        return jnp.sum(block * block, axis=1, keepdims=True)
+
+    def step(main, rest, state_row):
+        mean = (squares(main) + squares(rest)) * (1.0 / D)
+        state = as_column(state_row) + mean
+        root = jnp.sqrt(state)
+        wide = jnp.concatenate([root] * (MAIN // 128), axis=1)
+        return state, LEARN_RATE * main / wide, LEARN_RATE * rest / root
+
+    tables = (
+        (lhs, lhs_acc, lhs_grad, new_lhs, new_lhs_acc),
+        (rhs, rhs_acc, rhs_grad, new_rhs, new_rhs_acc),
+    )
+    turn[...] = jnp.zeros_like(turn)
+    for table, state_in, grad, new, new_state in tables:
+        rows = table.shape[0]
+        turn[:REST, :rows] = grad[rows:, :rows].astype(F32)
+        rest = jnp.transpose(turn[:, :rows])
+        state, main_step, rest_step = step(grad[:rows, :].astype(F32), rest, state_in[...])
+        new[:, :MAIN] = (table[:, :MAIN].astype(F32) - main_step).astype(BF)
+        new[:, MAIN:] = (table[:, MAIN:].astype(F32) - rest_step[:, :REST]).astype(BF)
+        new_state[...] = jnp.transpose(state)[:1, :]
+    states[...] = jnp.ones_like(states)
+    states[: operators.shape[0], :D] = operator_acc[...]
+    for r in range(operators.shape[0]):
+        turn[:REST, :MAIN] = oper_grad[r, D : D + REST, :].astype(F32)
+        turn[:REST, MAIN:] = oper_grad[r, D + REST : D + 2 * REST, :128].astype(F32)
+        rest = jnp.transpose(turn[...])
+        main = oper_grad[r].astype(F32)
+        state, main_step, rest_step = step(main, rest, states[r : r + 1, :])
+        new_operators[r, :, :MAIN] = operators[r, :, :MAIN] - main_step[:D]
+        new_operators[r, :, MAIN:] = operators[r, :, MAIN:] - rest_step[:D, :REST]
+        new_operator_acc[r : r + 1, :] = jnp.transpose(state)[:1, :D]
+
+
+def update(*arrays):
+    lhs, lhs_acc, _, rhs, rhs_acc, _, operators, operator_acc, _ = arrays
+    vmem = pl.BlockSpec(memory_space=pltpu.VMEM)
+    outs = (lhs, lhs_acc, rhs, rhs_acc, operators, operator_acc)
+    return pl.pallas_call(
+        update_kernel,
+        in_specs=[vmem] * 9,
+        out_specs=[vmem] * 6,
+        out_shape=[jax.ShapeDtypeStruct(x.shape, x.dtype) for x in outs],
+        scratch_shapes=[pltpu.VMEM((128, WIDE), F32), pltpu.VMEM((8, WIDE), F32)],
+        compiler_params=pltpu.CompilerParams(vmem_limit_bytes=32 * 1024 * 1024),
+        name="update",
+    )(*arrays)
 
 
 def per_device(
@@ -598,15 +702,16 @@
     lists, left_part, right_part = collect(partner_mask, packed, lhs_emb, rhs_emb)
     grad_left, grad_right, grad_oper = bucket(lists, left_part, right_part, operators)
     own_right, own_left, total_oper = reduce(partner_mask, grad_right, grad_left, grad_oper)
-    new_lhs, new_lhs_acc = row_adagrad(lhs_emb, lhs_acc, own_left)
-    new_rhs, new_rhs_acc = row_adagrad(rhs_emb, rhs_acc, own_right.astype(F32))
-    total_oper = total_oper.reshape(operators.shape[0], WIDE, D)[:, :D].astype(F32)
-    new_operators, new_operator_acc = row_adagrad(operators, operator_acc, total_oper)
+    as_row = lambda state: state.reshape(1, -1)
+    new_lhs, new_lhs_acc, new_rhs, new_rhs_acc, new_operators, new_operator_acc = update(
+        lhs_emb, as_row(lhs_acc), own_left, rhs_emb, as_row(rhs_acc), own_right,
+        operators, operator_acc, total_oper,
+    )
     return (
-        new_lhs.astype(BF),
-        new_lhs_acc,
-        new_rhs.astype(BF),
-        new_rhs_acc,
+        new_lhs,
+        new_lhs_acc.reshape(-1),
+        new_rhs,
+        new_rhs_acc.reshape(-1),
         new_operators,
         new_operator_acc,
     )

time: 115 us -> 97.7 us (0.85); the launches traced: 113 us -> 97.4 us
  Pallas kernels: 97 us -> 90.1 us
  other arithmetic: 6.06 us -> 1.47 us
  local copies, waits for them, and re-layouts: 7.75 us -> 3.79 us
    pallas_call x1, Pallas kernels: 18 us -> 10.2 us  [bucket(): pl.pallas_call(functools.partial(bucket_kernel, groups, total // groups),...]
    unnamed x16 -> x12, local copies, waits for them, and re-layouts: 7.75 us -> 3.79 us
    pallas_call x1, Pallas kernels: 30.4 us -> 26.9 us  [collect(): pl.pallas_call(functools.partial(collect_kernel, groups), in_specs=[pl.Bl...]
    pallas_call x0 -> x1, Pallas kernels: none -> 2.77 us  [update(): pl.pallas_call(update_kernel, in_specs=[vmem] * 9, out_specs=[vmem] * 6,...]
    sqrt x3 -> x0, other arithmetic: 1.73 us -> none  [row_adagrad(): jnp.sqrt(new_state)[..., None]]
    pallas_call x1, Pallas kernels: 48.6 us -> 50.2 us  [reduce(): pl.pallas_call(functools.partial(reduce_kernel, groups), in_specs=[pl.Blo...]
    sub x1 -> x0, other arithmetic: 1.45 us -> none  [row_adagrad(): weights_in.astype(F32)]
where the time goes in v3:
time: 97.7 us; the launch traced here: 97.4 us
  Pallas kernels  90.1 us (92%)
  local copies, waits for them, and re-layouts  3.79 us (4%)
  between operations  2.03 us (2%)
  other arithmetic  1.47 us (2%)
    pallas_call x1, Pallas kernels, reduce(): pl.pallas_call(functools.partial(reduce_kernel, groups), in_specs=[pl.Blo...  50.2 us
    pallas_call x1, Pallas kernels, collect(): pl.pallas_call(functools.partial(collect_kernel, groups), in_specs=[pl.Bl...  26.9 us
    pallas_call x1, Pallas kernels, bucket(): pl.pallas_call(functools.partial(bucket_kernel, groups, total // groups),...  10.2 us
    unnamed x12, local copies, waits for them, and re-layouts  3.79 us
    pallas_call x1, Pallas kernels, update(): pl.pallas_call(update_kernel, in_specs=[vmem] * 9, out_specs=[vmem] * 6,...  2.77 us

profile of v3, /device:TPU:0, one launch (start us, length us, event | category | flops | bytes accessed | tf_op | source)
XLA Modules:
  0.0 97.4 jit_solution(8862800056955603068)
XLA Ops:
  1.9 0.7 broadcast_select_fusion
  2.7 0.7 pad_add_fusion.lists
  3.4 1.1 %copy.20.left.lhs = bf16[256,400]{1,0:T(8,128)(2,1)S(1)} copy(bf16[256,400]{0,1:T(8,128)(2,1)} %param.12) | data formatting | bytes 409600 | tf_op args[0]
  4.5 1.1 %copy.19.right.rhs = bf16[256,400]{1,0:T(8,128)(2,1)S(1)} copy(bf16[256,400]{0,1:T(8,128)(2,1)} %param.14) | data formatting | bytes 409600 | tf_op args[2]
  5.5 26.9 %collect.1 = (s32[64,512]{1,0:T(8,128)S(1)}, bf16[1088,384]{1,0:T(8,128)(2,1)S(1)}, bf16[1088,384]{1,0:T(8,128)(2,1)S(1)}) custom-call(s32[1]{0:T(128)S(6)} %copy.24.mask, s32[16,512]{1,0:T(8,128)S(1)} %pad_add_fusion.lists, bf16[256,400]{1,0:T(8,128)(2,1)S(1)} %copy.20.left.lhs, bf16[256,400]{1,0:T(8,128)(2,1)S(1)} %copy.19.right.rhs), custom_call_target="tpu_custom_call" | custom-call | tf_op jit(solution)/shard_map/collect/pallas_call | solution.py:210
  32.5 10.2 %bucket.1 = (bf16[1088,384]{1,0:T(8,128)(2,1)S(1)}, bf16[1088,384]{1,0:T(8,128)(2,1)S(1)}, f32[2,512,384]{2,1,0:T(8,128)S(1)}) custom-call(s32[64,512]{1,0:T(8,128)S(1)} %get-tuple-element.21.info.index, s32[64,512]{1,0:T(8,128)S(1)} %get-tuple-element.21.info.index, bf16[1088,384]{1,0:T(8,128)(2,1)S(1)} %get-tuple-element.22.left_in, ...), custom_call_target="tpu_custom_call" | custom-call | tf_op jit(solution)/shard_map/bucket/pallas_call | solution.py:599
  42.7 0.0 copy-start
  42.7 0.0 copy-start.1
  42.7 0.0 copy-start.2
  42.7 0.0 copy-start.3
  42.7 50.2 %reduce.1 = (bf16[272,384]{1,0:T(8,128)(2,1)S(1)}, f32[272,384]{1,0:T(8,128)S(1)}, bf16[2,512,384]{2,1,0:T(8,128)(2,1)S(1)}) custom-call(s32[1]{0:T(128)S(6)} %copy.24.mask, bf16[1088,384]{1,0:T(8,128)(2,1)S(1)} %get-tuple-element.24.right, bf16[1088,384]{1,0:T(8,128)(2,1)S(1)} %get-tuple-element.25.left, f32[2,512,384]{2,1,0:T(8,128)S(1)} %get-tuple-element.26.oper), custom_call_target="tpu_custom_call" | custom-call | tf_op jit(solution)/shard_map/reduce/pallas_call | solution.py:417
  92.9 0.0 copy-done
  92.9 0.0 copy-done.1
  92.9 0.0 copy-done.2
  92.9 0.0 copy-done.3
  93.0 2.8 %update.1 = (bf16[256,400]{1,0:T(8,128)(2,1)S(1)}, f32[1,256]{1,0:T(1,128)}, bf16[256,400]{1,0:T(8,128)(2,1)S(1)}, f32[1,256]{1,0:T(1,128)}, f32[2,400,400]{2,1,0:T(8,128)}, /*index=5*/f32[2,400]{1,0:T(2,128)}) custom-call(bf16[256,400]{1,0:T(8,128)(2,1)S(1)} %copy.20.left.lhs, f32[1,256]{1,0:T(1,128)S(1)} %bitcast.6, ...), custom_call_target="tpu_custom_call" | custom-call | tf_op jit(solution)/shard_map/update/pallas_call | solution.py:673
  95.7 0.8 copy.22
  96.5 0.8 copy.23
  (1 shorter events, 0.0 us)
Async XLA Ops:
  42.7 50.3 %copy-start = (f32[2,400,400]{2,1,0:T(8,128)S(1)}, f32[2,400,400]{2,1,0:T(8,128)}, u32[]{:S(2)}) copy-start(f32[2,400,400]{2,1,0:T(8,128)} %operators.1) | copy-start | bytes 3840004
  42.7 50.2 %copy-start.1 = (f32[2,400]{1,0:T(2,128)S(1)}, f32[2,400]{1,0:T(2,128)}, u32[]{:S(2)}) copy-start(f32[2,400]{1,0:T(2,128)} %operator_acc.1) | copy-start | bytes 9604
  42.7 50.2 %copy-start.2 = (f32[256]{0:T(256)S(1)}, f32[256]{0:T(256)}, u32[]{:S(2)}) copy-start(f32[256]{0:T(256)} %param.13) | copy-start | bytes 3076
  42.7 50.2 %copy-start.3 = (f32[256]{0:T(256)S(1)}, f32[256]{0:T(256)}, u32[]{:S(2)}) copy-start(f32[256]{0:T(256)} %param.15) | copy-start | bytes 3076
